TPU v7x, 32 devices: a whole 2x2x4 slice. The times are simulated.
32 devices in a mesh: lat: 4 (over z), lon: 8 (over y, x, core).
Axes of the slice: x: 2, y: 2, z: 4, core: 2. Of those that a mesh axis runs over, the one named last changes fastest.
Arguments:
- depth: float32 [512, 4096], P('lat', 'lon'), may hold values from 0 to 1
- soakage: float32 [512, 4096], P('lat', 'lon'), may hold values from 0.05 to 0.5
- elevation: float32 [512, 4096], P('lat', 'lon'), may hold values from -6 to 6
- roughness: float32 [512, 4096], P('lat', 'lon'), may hold values from 1 to 3
- conductivity: float32 [512, 4096], P('lat', 'lon'), may hold values from 0.05 to 1
- runoff: float32 [4, 32], P('lat', 'lon'), may hold values from 0.2 to 2
- coarse_index: int32 [512, 4096], P('lat', 'lon'), may hold values from 0 to 17, as said below
- wet_tiles: int32 [8, 64], P('lat', 'lon'), may hold values from 0 to 1, as said below
- channel_reach: int32 [512, 4096], P('lat', 'lon'), may hold values from 0 to 8192, as said below
- block_order: int32 [64], replicated, may hold values from 0 to 63, each once
Outputs:
- depth_out: float32 [512, 4096], P('lat', 'lon')
- soakage_out: float32 [512, 4096], P('lat', 'lon')
- reach_inflow: float32 [64, 128], P(('lat', 'lon'))
Inputs may be any that keep to these rules, and one draw needn't show every extreme that they name: `coarse_index`: index into the device's runoff blocks with a rim of one block on each side, rows of 6 entries; the cell's block or one beside it. `wet_tiles`: 1 marks a wet tile. `channel_reach`: A reach index, or 8192 for a cell without a channel.
All inputs are finite; a program needn't handle non-finite values.
Results may differ from a plain program's by a relative error of at most 0.0001.
Values sent between devices are 32-bit elements; how exact they have to be, the bound alone decides.
A program may use at most 64 MiB of HBM per device.

v0:
```python
import jax
import jax.numpy as jnp
from jax import lax
from jax.sharding import PartitionSpec as P

TILE = 64
SUBSTEPS = 2
REACH_BLOCK = 128


time_step = 0.05
suction = 0.3
slope_floor = 0.25
drain_rate = 0.5


def with_halo(x, sides, width):
    for axis, dim in sides:
        size, length = (lax.axis_size(axis), x.shape[dim])
        up = [(i, (i + 1) % size) for i in range(size - 1)]
        down = [(j, i) for i, j in up]
        last = lax.slice_in_dim(x, length - width, length, axis=dim)
        first = lax.slice_in_dim(x, 0, width, axis=dim)
        before = lax.ppermute(last, axis, up)
        after = lax.ppermute(first, axis, down)
        x = jnp.concatenate([before, x, after], axis=dim)
    return x


def power_five_thirds(value):
    return value * jnp.cbrt(value * value)


def face_flux(
    left_depth, right_depth, left_elev, right_elev, left_rough, right_rough, left_wet, right_wet
):
    head_drop = left_elev + left_depth - (right_elev + right_depth)
    face_depth = 0.5 * (left_depth + right_depth)
    face_rough = 0.5 * (left_rough + right_rough)
    return (
        left_wet
        * right_wet
        * power_five_thirds(face_depth)
        / face_rough
        * head_drop
        / jnp.sqrt(jnp.abs(head_drop) + slope_floor)
    )


def outflow(depth_pad, elev_pad, rough_pad, wet_pad):
    eastward = face_flux(
        depth_pad[1:-1, :-1],
        depth_pad[1:-1, 1:],
        elev_pad[1:-1, :-1],
        elev_pad[1:-1, 1:],
        rough_pad[1:-1, :-1],
        rough_pad[1:-1, 1:],
        wet_pad[1:-1, :-1],
        wet_pad[1:-1, 1:],
    )
    southward = face_flux(
        depth_pad[:-1, 1:-1],
        depth_pad[1:, 1:-1],
        elev_pad[:-1, 1:-1],
        elev_pad[1:, 1:-1],
        rough_pad[:-1, 1:-1],
        rough_pad[1:, 1:-1],
        wet_pad[:-1, 1:-1],
        wet_pad[1:, 1:-1],
    )
    return eastward[:, 1:] - eastward[:, :-1] + southward[1:, :] - southward[:-1, :]


def shards(
    depth,
    soakage,
    elevation,
    roughness,
    conductivity,
    runoff,
    coarse_index,
    wet_tiles,
    channel_reach,
    block_order,
):
    num_reaches = block_order.shape[0] * REACH_BLOCK
    runoff_pad = with_halo(runoff, (("lat", 0), ("lon", 1)), 1)
    cell_rate = jnp.take(runoff_pad.reshape(-1), coarse_index)
    wet_cells = jnp.repeat(jnp.repeat(wet_tiles, TILE, 0), TILE, 1).astype(jnp.float32)
    channel = jnp.where(channel_reach < num_reaches, wet_cells, jnp.float32(0.0))
    stacked = jnp.stack([elevation, roughness, wet_cells])
    stacked_pad = with_halo(stacked, (("lat", 1), ("lon", 2)), 1)
    elev_pad = stacked_pad[0]
    rough_pad = stacked_pad[1]
    wet_pad = stacked_pad[2]
    flat_reach = channel_reach.reshape(-1)
    owned = jnp.zeros(
        (block_order.shape[0] // (lax.axis_size("lat") * lax.axis_size("lon")), REACH_BLOCK),
        jnp.float32,
    )
    level = depth
    soaked_sum = soakage
    for substep in range(SUBSTEPS):
        available = level + wet_cells * time_step * cell_rate
        potential = time_step * conductivity * (1.0 + suction / soaked_sum)
        soaked = wet_cells * jnp.minimum(potential, jnp.maximum(available, 0.0))
        ponded = available - soaked
        soaked_sum = soaked_sum + soaked
        depth_pad = with_halo(ponded, (("lat", 0), ("lon", 1)), 1)
        routed = ponded - time_step * outflow(depth_pad, elev_pad, rough_pad, wet_pad)
        drained = channel * time_step * drain_rate * power_five_thirds(routed) / roughness
        level = routed - drained
        partial_value = jax.ops.segment_sum(
            drained.reshape(-1), flat_reach, num_segments=num_reaches + 1
        )
        ordered = partial_value[:num_reaches].reshape(-1, REACH_BLOCK)[block_order]
        owned = owned + lax.psum_scatter(ordered, ("lat", "lon"), scatter_dimension=0, tiled=True)
    return (level, soaked_sum, owned)


def solution(mesh):
    placed = (
        P("lat", "lon"),
        P("lat", "lon"),
        P("lat", "lon"),
        P("lat", "lon"),
        P("lat", "lon"),
        P("lat", "lon"),
        P("lat", "lon"),
        P("lat", "lon"),
        P("lat", "lon"),
        P(),
    )
    return jax.shard_map(
        shards,
        mesh=mesh,
        in_specs=placed,
        out_specs=(P("lat", "lon"), P("lat", "lon"), P(("lat", "lon"), None)),
        check_vma=False,
    )
```

profile of v0, /device:TPU:0, one launch (start us, length us, event | category | flops | bytes accessed | tf_op | source)
XLA Modules:
  0.0 956.1 jit_solution(5111221045285524477)
XLA Ops:
  0.6 4.9 collective-permute-start
  5.6 1.3 collective-permute-start.1
  11.4 4.7 collective-permute-start.4
  16.3 1.4 collective-permute-start.5
  21.4 1.3 collective-permute-start.3
  22.7 3.5 collective-permute-done.3
  27.0 11.7 %add_subtract_fusion = f32[128,512]{0,1:T(8,128)S(1)} fusion(f32[128,512]{0,1:T(8,128)S(1)} %copy.49, f32[128,512]{0,1:T(8,128)S(1)} %copy.51, f32[128,512]{0,1:T(8,128)S(1)} %copy.50, f32[128,8]{0,1:T(8,128)S(1)} %convert_element_type.25, f32[]{:T(128)} %bitcast.18, f32[]{:T(128)} %bitcast.17, f32[]{:T(128)} %bitcast.16, f32[]{:T(128)} %bitcast.15, ...), kind=kLoop, calls=%fused_computation.60 | loop fusion | flops 3407872 | bytes 1314888 | tf_op jit(solution)/shard_map/sub | solution.py:107
  39.6 5.3 collective-permute-start.8
  47.6 4.0 collective-permute-start.6
  51.6 1.3 collective-permute-start.7
  52.9 2.2 collective-permute-done.9
  55.9 2.8 collective-permute-start.10
  58.7 1.3 collective-permute-start.11
  60.9 2.1 rsqrt_multiply_fusion.1
  63.0 1.7 rsqrt_multiply_fusion.3
  64.8 13.0 %add_add_fusion = (f32[128,512]{0,1:T(8,128)}, f32[128,512]{0,1:T(8,128)S(1)}, pred[128,512]{0,1:T(8,128)(4,1)S(1)}, f32[128,512]{0,1:T(8,128)}) fusion(f32[128,512]{0,1:T(8,128)S(1)} %copy.51, f32[128,512]{0,1:T(8,128)S(1)} %copy.50, f32[128,8]{0,1:T(8,128)S(1)} %convert_element_type.25, f32[128,512]{0,1:T(8,128)S(1)} %copy.49, f32[]{:T(128)} %bitcast.18, ...), kind=kLoop, calls=%fused_computation.59 | loop fusion | flops 4784128 | bytes 3739720 | tf_op jit(solution)/shard_map/add | solution.py:108
  78.6 12.9 %fusion.16 = f32[128,512]{0,1:T(8,128)S(1)} fusion(f32[128,512]{0,1:T(8,128)S(1)} %copy.51, f32[128,512]{0,1:T(8,128)S(1)} %copy.50, f32[128,8]{0,1:T(8,128)S(1)} %convert_element_type.25, f32[128,512]{0,1:T(8,128)} %get-tuple-element.15, f32[128,512]{0,1:T(8,128)} %copy-done.2, f32[128,512]{0,1:T(8,128)S(1)} %copy.49, f32[]{:T(128)} %bitcast.18, ...), kind=kLoop, calls=%fused_computation.83 | loop fusion | flops 3997696 | bytes 1839176 | tf_op jit(solution)/shard_map/sub | solution.py:107
  92.4 2.8 collective-permute-start.12
  95.2 1.3 collective-permute-start.13
  96.5 400.6 %scatter_custom_fusion = f32[8193]{0:T(1024)S(1)} fusion(s32[65536]{0:T(1024)} %bitcast.86, f32[65536]{0:T(1024)S(1)} %bitcast.89, f32[]{:T(128)} %constant.7.clone.1), kind=kCustom, calls=%fused_computation.65 | custom fusion | flops 65536 | bytes 33284 | tf_op jit(solution)/shard_map/scatter-add | solution.py:113
  498.7 3.9 collective-permute-start.14
  502.5 1.5 collective-permute-start.15
  507.5 400.6 %scatter_custom_fusion.1 = f32[8193]{0:T(1024)S(1)} fusion(s32[65536]{0:T(1024)} %bitcast.87, f32[65536]{0:T(1024)S(1)} %bitcast.88, f32[]{:T(128)} %constant.7.clone.1), kind=kCustom, calls=%fused_computation.63 | custom fusion | flops 65536 | bytes 33284 | tf_op jit(solution)/shard_map/scatter-add | solution.py:113
  908.7 46.0 %all-reduce = f32[64,128]{1,0:T(8,128)S(1)} all-reduce(f32[64,128]{1,0:T(8,128)S(1)} %add.133), channel_id=3, replica_groups=mesh['lat'=4,'lon'=8] {'lat','lon'}, use_global_device_ids=true, to_apply=%region_1.2.clone | all-reduce | flops 8192 | bytes 65536
  (90 shorter events, 23.0 us)
Async XLA Ops:
  0.6 19.3 %collective-permute-start = (f32[1,4]{1,0:T(1,128)}, f32[1,4]{1,0:T(1,128)S(1)}, u32[]{:S(2)}, u32[]{:S(2)}) collective-permute-start(f32[1,4]{1,0:T(1,128)} %param.15), channel_id=1, source_target_pairs={{0,8},{8,16},{16,24},{1,9},{9,17},{17,25},{2,10},{10,18},{18,26},{... | collective-permute-start | bytes 56 | tf_op jit(solution)/shard_map/ppermute | solution.py:24
  5.6 14.4 %collective-permute-start.1 = (f32[1,4]{1,0:T(1,128)}, f32[1,4]{1,0:T(1,128)S(1)}, u32[]{:S(2)}, u32[]{:S(2)}) collective-permute-start(f32[1,4]{1,0:T(1,128)} %param.15), channel_id=1, source_target_pairs={{8,0},{16,8},{24,16},{9,1},{17,9},{25,17},{10,2},{18,10},{26,18},{... | collective-permute-start | bytes 56 | tf_op jit(solution)/shard_map/ppermute | solution.py:25
  10.8 7.0 copy-start.7
  11.1 6.8 copy-start.8
  11.1 7.0 copy-start.9
  11.1 7.1 copy-start.10
  11.4 7.0 copy-start.5
  11.4 34.8 %collective-permute-start.4 = (f32[3,1,512]{2,1,0:T(1,128)S(1)}, f32[3,1,512]{2,1,0:T(1,128)S(1)}, u32[]{:S(2)}, u32[]{:S(2)}) collective-permute-start(f32[3,1,512]{2,1,0:T(1,128)S(1)} %copy.54), channel_id=1, source_target_pairs={{0,8},{8,16},{16,24},{1,9},{9,17},{17,25},{2,10},{10,18},{18,26},{... | collective-permute-start | bytes 18440 | tf_op jit(solution)/shard_map/ppermute | solution.py:24
  16.3 30.1 %collective-permute-start.5 = (f32[3,1,512]{2,1,0:T(1,128)S(1)}, f32[3,1,512]{2,1,0:T(1,128)S(1)}, u32[]{:S(2)}, u32[]{:S(2)}) collective-permute-start(f32[3,1,512]{2,1,0:T(1,128)S(1)} %copy.55), channel_id=1, source_target_pairs={{8,0},{16,8},{24,16},{9,1},{17,9},{25,17},{10,2},{18,10},{26,18},{... | collective-permute-start | bytes 18440 | tf_op jit(solution)/shard_map/ppermute | solution.py:25
  20.1 2.6 collective-permute-start.2
  21.4 4.8 collective-permute-start.3
  39.6 13.3 %collective-permute-start.8 = (f32[1,512]{0,1:T(8,128)}, f32[1,512]{0,1:T(8,128)}, u32[]{:S(2)}, u32[]{:S(2)}) collective-permute-start(f32[1,512]{0,1:T(8,128)} %get-tuple-element.31), channel_id=1, source_target_pairs={{0,8},{8,16},{16,24},{1,9},{9,17},{17,25},{2,10},{10,18},{18,26},{... | collective-permute-start | bytes 6152 | tf_op jit(solution)/shard_map/ppermute | solution.py:24
  44.8 10.3 %collective-permute-start.9 = (f32[1,512]{0,1:T(8,128)}, f32[1,512]{0,1:T(8,128)}, u32[]{:S(2)}, u32[]{:S(2)}) collective-permute-start(f32[1,512]{0,1:T(8,128)} %get-tuple-element.32), channel_id=1, source_target_pairs={{8,0},{16,8},{24,16},{9,1},{17,9},{25,17},{10,2},{18,10},{26,18},{... | collective-permute-start | bytes 6152 | tf_op jit(solution)/shard_map/ppermute | solution.py:25
  46.8 13.3 %copy-start.1 = (f32[128,8,64]{0,2,1:T(8,128)S(1)}, f32[128,8,64]{0,2,1:T(8,128)}, u32[]{:S(2)}) copy-start(f32[128,8,64]{0,2,1:T(8,128)} %copy-done) | copy-start | bytes 786436
  47.6 12.4 %collective-permute-start.6 = (f32[3,130,1]{1,2,0:T(1,128)S(1)}, f32[3,130,1]{1,2,0:T(1,128)S(1)}, u32[]{:S(2)}, u32[]{:S(2)}) collective-permute-start(f32[3,130,1]{1,2,0:T(1,128)S(1)} %get-tuple-element.18), channel_id=1, source_target_pairs={{0,1},{1,2},{2,3},{3,4},{4,5},{5,6},{6,7},{8,9},{9,10},{10,11},{11... | collective-permute-start | bytes 4688 | tf_op jit(solution)/shard_map/ppermute | solution.py:24
  51.6 8.4 collective-permute-start.7
  55.9 7.2 collective-permute-start.10
  58.7 4.3 collective-permute-start.11
  78.6 17.8 %copy-start.6 = (f32[128,512]{1,0:T(8,128)S(1)}, f32[128,512]{1,0:T(8,128)}, u32[]{:S(2)}) copy-start(f32[128,512]{1,0:T(8,128)} %copy.62) | copy-start | bytes 786436
  78.6 418.5 %copy-start.4 = (f32[128,512]{0,1:T(8,128)S(1)}, f32[128,512]{0,1:T(8,128)}, u32[]{:S(2)}) copy-start(f32[128,512]{0,1:T(8,128)} %get-tuple-element.12) | copy-start | bytes 786436
  92.4 406.2 %collective-permute-start.12 = (f32[1,512]{0,1:T(8,128)}, f32[1,512]{0,1:T(8,128)S(1)}, u32[]{:S(2)}, u32[]{:S(2)}) collective-permute-start(f32[1,512]{0,1:T(8,128)} %get-tuple-element.29), channel_id=1, source_target_pairs={{0,8},{8,16},{16,24},{1,9},{9,17},{17,25},{2,10},{10,18},{18,26},{... | collective-permute-start | bytes 6152 | tf_op jit(solution)/shard_map/ppermute | solution.py:24
  95.2 403.4 %collective-permute-start.13 = (f32[1,512]{0,1:T(8,128)S(1)}, f32[1,512]{0,1:T(8,128)S(1)}, u32[]{:S(2)}, u32[]{:S(2)}) collective-permute-start(f32[1,512]{0,1:T(8,128)S(1)} %get-tuple-element.30), channel_id=1, source_target_pairs={{8,0},{16,8},{24,16},{9,1},{17,9},{25,17},{10,2},{18,10},{26,18},{... | collective-permute-start | bytes 6152 | tf_op jit(solution)/shard_map/ppermute | solution.py:25
  498.7 6.5 collective-permute-start.14
  502.5 3.7 collective-permute-start.15
  (5 other events, 10.6 us)
where the time goes:
time: 957 us; the launch traced here: 956 us
  other arithmetic  848 us (89%)
  blocking collectives  46 us (5%)
  starting transfers between devices  40.2 us (4%)
  local copies, waits for them, and re-layouts  13.9 us (1%)
    scatter-add x2, other arithmetic, shards(): jax.ops.segment_sum(drained.reshape(-1), flat_reach, num_segments=num_rea...  801 us
    unnamed x1, blocking collectives  46 us
    ppermute x8, starting transfers between devices, with_halo(): before = lax.ppermute(last, axis, up)  29.6 us
    sub x2, other arithmetic, shards(): ponded = available - soaked  24.6 us
  transfers between devices with their start and end apart: 16, of which 3 were waited for; matrix products, arithmetic and copies ran while one was open for 45% of the time, Pallas kernels for 0%

commit v1 on v0

v1 whole, which is shorter than its diff:
```python
import functools
import math

import jax
import jax.numpy as jnp
from jax import lax
from jax.experimental import pallas as pl
from jax.experimental.pallas import tpu as pltpu
from jax.sharding import PartitionSpec as P

TILE = 64
REACH_BLOCK = 128
LANES = 128
BAND = 8
PACK = 16
MESH = pl.DeviceIdType.MESH

time_step = 0.05
suction = 0.3
slope_floor = 0.25
drain_rate = 0.5

FACE_SCALE = time_step * 2.0 * 0.5 ** (5.0 / 3.0)

STEPS = ((-1, 0), (1, 0), (0, -1), (0, 1), (-1, -1), (-1, 1), (1, -1), (1, 1))
OPPOSITE = (1, 0, 3, 2, 7, 6, 5, 4)
ELEV, ROUGH, WET, RATE = range(4)


def power_five_thirds(value):
    return value * jnp.exp2(jnp.log(value * value) * (1.0 / (3.0 * math.log(2.0))))


def face_flux(coef, depth_sum, head_drop):
    return (
        coef
        * power_five_thirds(depth_sum)
        * (head_drop * lax.rsqrt(jnp.abs(head_drop) + slope_floor))
    )


def infiltrate(level, soaked_sum, conductivity, supply, wet):
    available = level + supply
    potential = time_step * conductivity * (1.0 + suction / soaked_sum)
    soaked = wet * jnp.minimum(potential, jnp.maximum(available, 0.0))
    return available - soaked, soaked_sum + soaked


def kernel(
    n_lat,
    n_lon,
    depth,
    soakage,
    elevation,
    roughness,
    conductivity,
    runoff,
    coarse,
    wet_tiles,
    reach,
    order,
    depth_out,
    soak_out,
    inflow_out,
    wet_rows,
    ponded,
    resid,
    supply,
    coef_e,
    coef_s,
    coef_d,
    drained_sum,
    own_edge,
    near_edge,
    near_corner,
    own_depth,
    near_depth,
    totals,
    arrived,
    edge_send,
    edge_recv,
    depth_send,
    depth_recv,
    total_send,
    total_recv,
):
    rows, cols = depth.shape
    bands = rows // BAND
    chunks = cols // LANES
    blocks = order.shape[0]
    n_dev = n_lat * n_lon
    per_dev = blocks // n_dev
    num_reaches = blocks * REACH_BLOCK
    lat, lon = lax.axis_index("lat"), lax.axis_index("lon")
    me = lat * n_lon + lon

    near_edge[...] = jnp.zeros_like(near_edge)
    near_corner[...] = jnp.zeros_like(near_corner)
    near_depth[...] = jnp.zeros_like(near_depth)

    barrier = pltpu.get_barrier_semaphore()

    def other(offset):
        device = lax.rem(me + offset, n_dev)
        return (lax.div(device, n_lon), lax.rem(device, n_lon))

    @pl.loop(1, n_dev)
    def _(offset):
        pl.semaphore_signal(barrier, inc=1, device_id=other(offset), device_id_type=MESH)

    def on_side(side, action):
        up, right = STEPS[side]
        row, col = lat + up, lon + right
        inside = (row >= 0) & (row < n_lat) & (col >= 0) & (col < n_lon)

        @pl.when(inside)
        def _():
            action((row, col))

    def edge_copy(side, device, slot):
        if side < 4:
            src, dst = own_edge.at[side], near_edge.at[slot]
        else:
            src, dst = own_edge.at[0, RATE], near_corner.at[slot - 4]
        return pltpu.make_async_remote_copy(
            src_ref=src,
            dst_ref=dst,
            send_sem=edge_send.at[side],
            recv_sem=edge_recv.at[slot],
            device_id=device,
            device_id_type=MESH,
        )

    def depth_copy(step, side, device, slot):
        return pltpu.make_async_remote_copy(
            src_ref=own_depth.at[step, side],
            dst_ref=near_depth.at[step, slot],
            send_sem=depth_send.at[step, side],
            recv_sem=depth_recv.at[step, slot],
            device_id=device,
            device_id_type=MESH,
        )

    def total_copy(offset):
        device = lax.rem(me + offset, n_dev)
        return pltpu.make_async_remote_copy(
            src_ref=totals.at[device],
            dst_ref=arrived.at[offset],
            send_sem=total_send.at[offset],
            recv_sem=total_recv.at[offset],
            device_id=(lax.div(device, n_lon), lax.rem(device, n_lon)),
            device_id_type=MESH,
        )

    lane = lax.broadcasted_iota(jnp.int32, (BAND, LANES), 1)
    wide_lane = lax.broadcasted_iota(jnp.int32, (BAND, cols), 1)
    wide_row = lax.broadcasted_iota(jnp.int32, (BAND, cols), 0)
    square_row = lax.broadcasted_iota(jnp.int32, (rows, LANES), 0)
    square_lane = lax.broadcasted_iota(jnp.int32, (rows, LANES), 1)
    diagonal = square_row == square_lane

    def band_at(ref, b):
        return ref[pl.ds(pl.multiple_of(b * BAND, BAND), BAND), :]

    def put_band(ref, b, value):
        ref[pl.ds(pl.multiple_of(b * BAND, BAND), BAND), :] = value

    def wet_at(b):
        return band_at(wet_rows, lax.div(b, TILE // BAND))

    def below(here, after):
        return pltpu.roll(jnp.where(wide_row == 0, after, here), BAND - 1, 0)

    def above(before, here):
        return pltpu.roll(jnp.where(wide_row == BAND - 1, before, here), 1, 0)

    def east(here):
        return pltpu.roll(here, cols - 1, 1)

    def west(here):
        return pltpu.roll(here, 1, 1)

    def as_row(column):
        return jnp.sum(jnp.where(diagonal, column, 0.0), axis=0, keepdims=True)

    def as_column(row):
        return jnp.sum(jnp.where(diagonal, row, 0.0), axis=1, keepdims=True)

    def pack_edges(ref, put):
        for c in range(chunks):
            cut = slice(c * LANES, (c + 1) * LANES)
            put(0, c, ref[0:1, cut])
            put(1, c, ref[rows - 1 : rows, cut])
        put(2, 0, as_row(ref[:, 0:LANES][:, 0:1]))
        put(3, 0, as_row(ref[:, cols - LANES : cols][:, LANES - 1 : LANES]))

    tile_rows, tile_cols = wet_tiles.shape
    for tr in range(tile_rows):
        value = jnp.zeros((BAND, cols), jnp.float32)
        for tc in range(tile_cols):
            inside = (wide_lane >= tc * TILE) & (wide_lane < (tc + 1) * TILE)
            value = jnp.where(inside, wet_tiles[tr, tc].astype(jnp.float32), value)
        wet_rows[tr * BAND : (tr + 1) * BAND, :] = value

    own_edge[...] = jnp.zeros_like(own_edge)
    own_depth[...] = jnp.zeros_like(own_depth)

    def put_field(field):
        def put(side, line, value):
            own_edge[side, field, line : line + 1, :] = value

        return put

    pack_edges(elevation, put_field(ELEV))
    pack_edges(roughness, put_field(ROUGH))
    last_tile = (tile_rows - 1) * BAND
    for c in range(chunks):
        cut = slice(c * LANES, (c + 1) * LANES)
        own_edge[0, WET, c : c + 1, :] = wet_rows[0:1, cut]
        own_edge[1, WET, c : c + 1, :] = wet_rows[last_tile : last_tile + 1, cut]
    row_lane = lax.broadcasted_iota(jnp.int32, (1, LANES), 1)
    for side, tc in ((2, 0), (3, tile_cols - 1)):
        value = jnp.zeros((1, LANES), jnp.float32)
        for tr in range(tile_rows):
            inside = (row_lane >= tr * TILE) & (row_lane < (tr + 1) * TILE)
            value = jnp.where(inside, wet_tiles[tr, tc].astype(jnp.float32), value)
        own_edge[side, WET, 0:1, :] = value
    block_cols = runoff.shape[1]
    rates = jnp.zeros((BAND, LANES), jnp.float32)
    for c in range(block_cols):
        rates = jnp.where(lane == c, runoff[0, c], rates)
    for side in range(4):
        own_edge[side, RATE] = rates

    pl.semaphore_wait(barrier, n_dev - 1)
    for side in range(8):
        on_side(side, lambda device, side=side: edge_copy(side, device, OPPOSITE[side]).start())

    @pl.loop(0, bands)
    def _(b):
        after = jnp.minimum(b + 1, bands - 1)
        rough, wet = band_at(roughness, b), wet_at(b)
        rough_s = below(rough, band_at(roughness, after))
        wet_s = below(wet, wet_at(after))
        value = FACE_SCALE * wet * wet_s / (rough + rough_s)
        put_band(coef_s, b, jnp.where(wide_row + b * BAND == rows - 1, 0.0, value))
        value = FACE_SCALE * wet * east(wet) / (rough + east(rough))
        put_band(coef_e, b, jnp.where(wide_lane == cols - 1, 0.0, value))
        channel = jnp.where(band_at(reach, b) < num_reaches, wet, 0.0)
        put_band(coef_d, b, channel * (time_step * drain_rate) / rough)

    for side in range(8):
        on_side(side, lambda device, side=side: edge_copy(side, device, side).wait_recv())

    def entry(ref_tile, c):
        return jnp.broadcast_to(ref_tile[0:1, c : c + 1], (BAND, cols))

    def rate_row(left, middle, right):
        return (
            [entry(left, block_cols - 1)]
            + [entry(middle, c) for c in range(block_cols)]
            + [entry(right, 0)]
        )

    table = (
        rate_row(near_corner[0], near_edge[0, RATE], near_corner[1])
        + rate_row(near_edge[2, RATE], rates, near_edge[3, RATE])
        + rate_row(near_corner[2], near_edge[1, RATE], near_corner[3])
    )

    @pl.loop(0, bands)
    def _(b):
        index = band_at(coarse, b)
        wet = wet_at(b)
        rate = table[0]
        for k in range(1, len(table)):
            rate = jnp.where(index == k, table[k], rate)
        water = wet * time_step * rate
        put_band(supply, b, water)
        h, soaked = infiltrate(
            band_at(depth, b), band_at(soakage, b), band_at(conductivity, b), water, wet
        )
        put_band(ponded, b, h)
        put_band(soak_out, b, soaked)

    edge_rough = jnp.maximum(own_edge[:, ROUGH] + near_edge[:, ROUGH], 1.0)
    edge_coef = FACE_SCALE * own_edge[:, WET] * near_edge[:, WET] / edge_rough
    edge_drop = own_edge[:, ELEV] - near_edge[:, ELEV]

    def send_depth(step):
        def put(side, line, value):
            own_depth[step, side, line : line + 1, :] = value

        pack_edges(ponded, put)
        for side in range(4):
            on_side(
                side,
                lambda device, side=side: depth_copy(step, side, device, OPPOSITE[side]).start(),
            )

    def route(step):
        def body(b, flux_n):
            after = jnp.minimum(b + 1, bands - 1)
            h, h_after = band_at(ponded, b), band_at(ponded, after)
            head = band_at(elevation, b) + h
            head_after = band_at(elevation, after) + h_after
            flux_s = face_flux(
                band_at(coef_s, b), h + below(h, h_after), head - below(head, head_after)
            )
            flux_e = face_flux(band_at(coef_e, b), h + east(h), head - east(head))
            out = flux_e - west(flux_e) + flux_s - above(flux_n, flux_s)
            put_band(resid, b, h - out)
            return flux_s

        lax.fori_loop(0, bands, body, jnp.zeros((BAND, cols), jnp.float32))
        for side in range(4):
            on_side(
                side, lambda device, side=side: depth_copy(step, side, device, side).wait_recv()
            )
        mine, theirs = own_depth[step], near_depth[step]
        out = face_flux(edge_coef, mine + theirs, edge_drop + (mine - theirs))
        for c in range(chunks):
            cut = slice(c * LANES, (c + 1) * LANES)
            resid[0:1, cut] = resid[0:1, cut] - out[0, c : c + 1, :]
            resid[rows - 1 : rows, cut] = resid[rows - 1 : rows, cut] - out[1, c : c + 1, :]
        first, last = slice(0, LANES), slice(cols - LANES, cols)
        column = as_column(out[2, 0:1, :])
        resid[:, first] = resid[:, first] - jnp.where(square_lane == 0, column, 0.0)
        column = as_column(out[3, 0:1, :])
        resid[:, last] = resid[:, last] - jnp.where(square_lane == LANES - 1, column, 0.0)

    send_depth(0)
    route(0)

    @pl.loop(0, bands)
    def _(b):
        routed = band_at(resid, b)
        drained = band_at(coef_d, b) * power_five_thirds(routed)
        put_band(drained_sum, b, drained)
        h, soaked = infiltrate(
            routed - drained,
            band_at(soak_out, b),
            band_at(conductivity, b),
            band_at(supply, b),
            wet_at(b),
        )
        put_band(ponded, b, h)
        put_band(soak_out, b, soaked)

    send_depth(1)
    route(1)

    pack_row = lax.broadcasted_iota(jnp.int32, (PACK, LANES), 0)
    lines = [
        (pack_row + t * PACK).astype(jnp.float32).astype(jnp.bfloat16)
        for t in range(REACH_BLOCK // PACK)
    ]
    owners = []
    for t in range(blocks // PACK):
        value = jnp.zeros((PACK, LANES), jnp.int32)
        for i in range(PACK):
            value = jnp.where(pack_row == i, order[t * PACK + i], value)
        owners.append(value.astype(jnp.float32).astype(jnp.bfloat16))
    one = jnp.ones((PACK, LANES), jnp.bfloat16)
    zero = jnp.zeros((PACK, LANES), jnp.bfloat16)

    def drain(b, total):
        routed = band_at(resid, b)
        drained = band_at(coef_d, b) * power_five_thirds(routed)
        put_band(depth_out, b, routed - drained)
        value = band_at(drained_sum, b) + drained
        upper = value.astype(jnp.bfloat16).astype(jnp.float32)
        lower = value - upper
        cell = band_at(reach, b)
        block = lax.shift_right_logical(cell, 7).astype(jnp.float32)
        line = lax.bitwise_and(cell, REACH_BLOCK - 1).astype(jnp.float32)
        for i in range(BAND):

            def spread(x, c):
                row = x[i : i + 1, c * LANES : (c + 1) * LANES]
                return jnp.broadcast_to(row, (PACK, LANES)).astype(jnp.bfloat16)

            left, right = [], []
            for c in range(chunks):
                block_c, line_c = spread(block, c), spread(line, c)
                upper_c, lower_c = spread(upper, c), spread(lower, c)
                hits = [block_c == o for o in owners]
                left.append(
                    jnp.concatenate(
                        [jnp.where(hit, upper_c, zero) for hit in hits]
                        + [jnp.where(hit, lower_c, zero) for hit in hits],
                        axis=0,
                    )
                )
                right.append(
                    jnp.concatenate([jnp.where(line_c == o, one, zero) for o in lines], axis=0)
                )
            total = total + lax.dot_general(
                jnp.concatenate(left, axis=1),
                jnp.concatenate(right, axis=1),
                (((1,), (1,)), ((), ())),
                preferred_element_type=jnp.float32,
            )
        return total

    total = lax.fori_loop(
        0, bands, drain, jnp.zeros((2 * blocks, REACH_BLOCK), jnp.float32)
    )
    total = total[:blocks] + total[blocks:]
    for d in range(n_dev):
        totals[d] = total[d * per_dev : (d + 1) * per_dev]

    @pl.loop(1, n_dev)
    def _(offset):
        total_copy(offset).start()

    arrived[0] = totals[me]

    for side in range(8):
        on_side(side, lambda device, side=side: edge_copy(side, device, side).wait_send())
    for step in range(2):
        for side in range(4):
            on_side(
                side,
                lambda device, side=side, step=step: depth_copy(
                    step, side, device, side
                ).wait_send(),
            )

    @pl.loop(1, n_dev)
    def _(offset):
        total_copy(offset).wait_recv()

    inflow_out[...] = jnp.sum(arrived[...], axis=0)

    @pl.loop(1, n_dev)
    def _(offset):
        total_copy(offset).wait_send()


def shards(n_lat, n_lon, *operands):
    depth, order = operands[0], operands[9]
    rows, cols = depth.shape
    tile_rows = operands[7].shape[0]
    n_dev = n_lat * n_lon
    per_dev = order.shape[0] // n_dev
    vmem, smem = pl.BlockSpec(memory_space=pltpu.VMEM), pl.BlockSpec(memory_space=pltpu.SMEM)
    grid = pltpu.VMEM((rows, cols), jnp.float32)
    return pl.pallas_call(
        functools.partial(kernel, n_lat, n_lon),
        out_shape=(
            jax.ShapeDtypeStruct((rows, cols), jnp.float32),
            jax.ShapeDtypeStruct((rows, cols), jnp.float32),
            jax.ShapeDtypeStruct((per_dev, REACH_BLOCK), jnp.float32),
        ),
        in_specs=[vmem] * 5 + [smem, vmem, smem, vmem, smem],
        out_specs=(vmem, vmem, vmem),
        scratch_shapes=[
            pltpu.VMEM((tile_rows * BAND, cols), jnp.float32),
            grid,
            grid,
            grid,
            grid,
            grid,
            grid,
            grid,
            pltpu.VMEM((4, 4, BAND, LANES), jnp.float32),
            pltpu.VMEM((4, 4, BAND, LANES), jnp.float32),
            pltpu.VMEM((4, BAND, LANES), jnp.float32),
            pltpu.VMEM((2, 4, BAND, LANES), jnp.float32),
            pltpu.VMEM((2, 4, BAND, LANES), jnp.float32),
            pltpu.VMEM((n_dev, per_dev, REACH_BLOCK), jnp.float32),
            pltpu.VMEM((n_dev, per_dev, REACH_BLOCK), jnp.float32),
            pltpu.SemaphoreType.DMA((8,)),
            pltpu.SemaphoreType.DMA((8,)),
            pltpu.SemaphoreType.DMA((2, 4)),
            pltpu.SemaphoreType.DMA((2, 4)),
            pltpu.SemaphoreType.DMA((n_dev,)),
            pltpu.SemaphoreType.DMA((n_dev,)),
        ],
        compiler_params=pltpu.CompilerParams(
            collective_id=0, has_side_effects=True, vmem_limit_bytes=40 * 1024 * 1024
        ),
        name="flow",
    )(*operands)


def solution(mesh):
    placed = (P("lat", "lon"),) * 9 + (P(),)
    return jax.shard_map(
        functools.partial(shards, mesh.shape["lat"], mesh.shape["lon"]),
        mesh=mesh,
        in_specs=placed,
        out_specs=(P("lat", "lon"), P("lat", "lon"), P(("lat", "lon"), None)),
        check_vma=False,
    )
```

time: 957 us -> 41.2 us (0.04)
  other arithmetic: 848 us -> 0 us
  blocking collectives: 46 us -> 0 us
  starting transfers between devices: 40.2 us -> 0 us
  Pallas kernels: 0 us -> 29.6 us
    scatter-add x2 -> x0, other arithmetic: 801 us -> none  [shards(): jax.ops.segment_sum(drained.reshape(-1), flat_reach, num_segments=num_rea...]
    unnamed x1 -> x0, blocking collectives: 46 us -> none
    ppermute x16 -> x0, starting transfers between devices: 40.2 us -> none  [the longest x8 29.6 us: with_halo(): before = lax.ppermute(last, axis, up)]
    pallas_call x0 -> x1, Pallas kernels: none -> 29.6 us  [shards(): pl.pallas_call(functools.partial(kernel, n_lat, n_lon), out_shape=(jax.Sh...]
    sub x3 -> x0, other arithmetic: 25 us -> none  [the longest x2 24.6 us: shards(): ponded = available - soaked]
    add x2 -> x0, other arithmetic: 13 us -> none  [the longest x1 13 us: shards(): soaked_sum = soaked_sum + soaked]
  transfers between devices with their start and end apart: 16 -> 0, of which waited for: 3 -> 0; matrix products, arithmetic and copies ran while one was open for 45% -> 0% of each run, Pallas kernels for 0% -> 0%
where the time goes in v1:
time: 41.2 us; the launch traced here: 40.8 us
  Pallas kernels  29.6 us (72%)
  local copies, waits for them, and re-layouts  10.6 us (26%)
  between operations  0.66 us (2%)
    pallas_call x1, Pallas kernels, shards(): pl.pallas_call(functools.partial(kernel, n_lat, n_lon), out_shape=(jax.Sh...  29.6 us
    unnamed x23, local copies, waits for them, and re-layouts  10.6 us

profile of v1, /device:TPU:0, one launch (start us, length us, event | category | flops | bytes accessed | tf_op | source)
XLA Modules:
  0.0 40.8 jit_solution(14114082380732228449)
XLA Ops:
  0.6 0.0 copy-start
  0.6 0.9 %copy-done = f32[128,512]{1,0:T(8,128)S(1)} copy-done((f32[128,512]{1,0:T(8,128)S(1)}, f32[128,512]{1,0:T(8,128)}, u32[]{:S(2)}) %copy-start) | copy-done | bytes 262168
  1.6 0.0 copy-start.1
  1.6 0.9 %copy-done.1 = f32[128,512]{1,0:T(8,128)S(1)} copy-done((f32[128,512]{1,0:T(8,128)S(1)}, f32[128,512]{1,0:T(8,128)}, u32[]{:S(2)}) %copy-start.1) | copy-done | bytes 262168
  2.5 0.0 copy-start.2
  2.5 0.9 %copy-done.2 = f32[128,512]{1,0:T(8,128)S(1)} copy-done((f32[128,512]{1,0:T(8,128)S(1)}, f32[128,512]{1,0:T(8,128)}, u32[]{:S(2)}) %copy-start.2) | copy-done | bytes 262168
  3.5 0.0 copy-start.3
  3.5 0.9 %copy-done.3 = f32[128,512]{1,0:T(8,128)S(1)} copy-done((f32[128,512]{1,0:T(8,128)S(1)}, f32[128,512]{1,0:T(8,128)}, u32[]{:S(2)}) %copy-start.3) | copy-done | bytes 262168
  4.4 0.0 copy-start.4
  4.4 0.9 %copy-done.4 = f32[128,512]{1,0:T(8,128)S(1)} copy-done((f32[128,512]{1,0:T(8,128)S(1)}, f32[128,512]{1,0:T(8,128)}, u32[]{:S(2)}) %copy-start.4) | copy-done | bytes 262168
  5.4 0.0 copy-start.5
  5.4 0.9 %copy-done.5 = s32[128,512]{1,0:T(8,128)S(1)} copy-done((s32[128,512]{1,0:T(8,128)S(1)}, s32[128,512]{1,0:T(8,128)}, u32[]{:S(2)}) %copy-start.5) | copy-done | bytes 262168
  6.3 0.0 copy-start.6
  6.3 0.9 %copy-done.6 = s32[128,512]{1,0:T(8,128)S(1)} copy-done((s32[128,512]{1,0:T(8,128)S(1)}, s32[128,512]{1,0:T(8,128)}, u32[]{:S(2)}) %copy-start.6) | copy-done | bytes 262168
  7.3 0.0 copy-start.7
  7.3 0.7 %copy-done.7 = s32[2,8]{1,0:T(2,128)S(1)} copy-done((s32[2,8]{1,0:T(2,128)S(1)}, s32[2,8]{1,0:T(2,128)}, u32[]{:S(2)}) %copy-start.7) | copy-done | bytes 88
  8.0 0.0 copy-start.8
  8.0 0.7 %copy-done.8 = f32[1,4]{1,0:T(1,128)S(1)} copy-done((f32[1,4]{1,0:T(1,128)S(1)}, f32[1,4]{1,0:T(1,128)}, u32[]{:S(2)}) %copy-start.8) | copy-done | bytes 40
  8.6 0.0 copy-start.9
  8.6 0.7 %copy-done.9 = s32[64]{0:T(128)S(1)} copy-done((s32[64]{0:T(128)S(1)}, s32[64]{0:T(128)}, u32[]{:S(2)}) %copy-start.9) | copy-done | bytes 280
  9.3 29.6 %flow.1 = (f32[128,512]{1,0:T(8,128)S(1)}, f32[128,512]{1,0:T(8,128)S(1)}, f32[2,128]{1,0:T(2,128)S(1)}) custom-call(f32[128,512]{1,0:T(8,128)S(1)} %copy-done, f32[128,512]{1,0:T(8,128)S(1)} %copy-done.1, f32[128,512]{1,0:T(8,128)S(1)} %copy-done.2, f32[128,512]{1,0:T(8,128)S(1)} %copy-done.3, f32[128,512]{1,0:T(8,128)S(1)} %copy-done.4, ...), custom_call_target="tpu_custom_call" | custom-call | tf_op jit(solution)/shard_map/flow/pallas_call | solution.py:449
  38.8 0.7 %copy.16 = f32[128,512]{1,0:T(8,128)} copy(f32[128,512]{1,0:T(8,128)S(1)} %get-tuple-element.6) | data formatting | bytes 524288
  39.5 0.7 %copy.17 = f32[128,512]{1,0:T(8,128)} copy(f32[128,512]{1,0:T(8,128)S(1)} %get-tuple-element.7) | data formatting | bytes 524288
  40.3 0.6 %copy.18 = f32[2,128]{1,0:T(2,128)} copy(f32[2,128]{1,0:T(2,128)S(1)} %get-tuple-element.8) | data formatting | bytes 2048
Async XLA Ops:
  0.6 1.0 %copy-start = (f32[128,512]{1,0:T(8,128)S(1)}, f32[128,512]{1,0:T(8,128)}, u32[]{:S(2)}) copy-start(f32[128,512]{1,0:T(8,128)} %depth.1) | copy-start | bytes 786436
  1.6 0.9 %copy-start.1 = (f32[128,512]{1,0:T(8,128)S(1)}, f32[128,512]{1,0:T(8,128)}, u32[]{:S(2)}) copy-start(f32[128,512]{1,0:T(8,128)} %soakage.1) | copy-start | bytes 786436
  2.5 0.9 %copy-start.2 = (f32[128,512]{1,0:T(8,128)S(1)}, f32[128,512]{1,0:T(8,128)}, u32[]{:S(2)}) copy-start(f32[128,512]{1,0:T(8,128)} %elevation.1) | copy-start | bytes 786436
  3.5 0.9 %copy-start.3 = (f32[128,512]{1,0:T(8,128)S(1)}, f32[128,512]{1,0:T(8,128)}, u32[]{:S(2)}) copy-start(f32[128,512]{1,0:T(8,128)} %roughness.1) | copy-start | bytes 786436
  4.4 0.9 %copy-start.4 = (f32[128,512]{1,0:T(8,128)S(1)}, f32[128,512]{1,0:T(8,128)}, u32[]{:S(2)}) copy-start(f32[128,512]{1,0:T(8,128)} %conductivity.1) | copy-start | bytes 786436
  5.4 0.9 %copy-start.5 = (s32[128,512]{1,0:T(8,128)S(1)}, s32[128,512]{1,0:T(8,128)}, u32[]{:S(2)}) copy-start(s32[128,512]{1,0:T(8,128)} %coarse.1) | copy-start | bytes 786436
  6.3 0.9 %copy-start.6 = (s32[128,512]{1,0:T(8,128)S(1)}, s32[128,512]{1,0:T(8,128)}, u32[]{:S(2)}) copy-start(s32[128,512]{1,0:T(8,128)} %reach.1) | copy-start | bytes 786436
  7.3 0.7 %copy-start.7 = (s32[2,8]{1,0:T(2,128)S(1)}, s32[2,8]{1,0:T(2,128)}, u32[]{:S(2)}) copy-start(s32[2,8]{1,0:T(2,128)} %wet_tiles.1) | copy-start | bytes 196
  8.0 0.7 %copy-start.8 = (f32[1,4]{1,0:T(1,128)S(1)}, f32[1,4]{1,0:T(1,128)}, u32[]{:S(2)}) copy-start(f32[1,4]{1,0:T(1,128)} %runoff.1) | copy-start | bytes 52
  8.6 0.7 %copy-start.9 = (s32[64]{0:T(128)S(1)}, s32[64]{0:T(128)}, u32[]{:S(2)}) copy-start(s32[64]{0:T(128)} %order.1) | copy-start | bytes 772

commit v2 on v1

--- a/solution.py
+++ b/solution.py
@@ -13,6 +13,7 @@
 LANES = 128
 BAND = 8
 PACK = 16
+VMEM_LIMIT = 60 * 1024 * 1024
 MESH = pl.DeviceIdType.MESH
 
 time_step = 0.05
@@ -49,6 +50,19 @@
 def kernel(
     n_lat,
     n_lon,
+    depth_hbm,
+    soakage_hbm,
+    elevation_hbm,
+    roughness_hbm,
+    conductivity_hbm,
+    runoff_hbm,
+    coarse_hbm,
+    wet_tiles_hbm,
+    reach_hbm,
+    order_hbm,
+    depth_out_hbm,
+    soak_out_hbm,
+    inflow_out_hbm,
     depth,
     soakage,
     elevation,
@@ -62,6 +76,8 @@
     depth_out,
     soak_out,
     inflow_out,
+    load_sem,
+    save_sem,
     wet_rows,
     ponded,
     resid,
@@ -94,6 +110,25 @@
     lat, lon = lax.axis_index("lat"), lax.axis_index("lon")
     me = lat * n_lon + lon
 
+    loads = [
+        pltpu.make_async_copy(src, dst, load_sem.at[k])
+        for k, (src, dst) in enumerate(
+            (
+                (wet_tiles_hbm, wet_tiles),
+                (runoff_hbm, runoff),
+                (elevation_hbm, elevation),
+                (roughness_hbm, roughness),
+                (reach_hbm, reach),
+                (order_hbm, order),
+                (coarse_hbm, coarse),
+                (depth_hbm, depth),
+                (soakage_hbm, soakage),
+                (conductivity_hbm, conductivity),
+            )
+        )
+    ]
+    for load in loads:
+        load.start()
     near_edge[...] = jnp.zeros_like(near_edge)
     near_corner[...] = jnp.zeros_like(near_corner)
     near_depth[...] = jnp.zeros_like(near_depth)
@@ -193,6 +228,9 @@
             put(1, c, ref[rows - 1 : rows, cut])
         put(2, 0, as_row(ref[:, 0:LANES][:, 0:1]))
         put(3, 0, as_row(ref[:, cols - LANES : cols][:, LANES - 1 : LANES]))
+
+    for load in loads[:4]:
+        load.wait()
 
     tile_rows, tile_cols = wet_tiles.shape
     for tr in range(tile_rows):
@@ -236,7 +274,10 @@
     for side in range(8):
         on_side(side, lambda device, side=side: edge_copy(side, device, OPPOSITE[side]).start())
 
-    @pl.loop(0, bands)
+    for load in loads[4:]:
+        load.wait()
+
+    @pl.loop(0, bands, unroll=2)
     def _(b):
         after = jnp.minimum(b + 1, bands - 1)
         rough, wet = band_at(roughness, b), wet_at(b)
@@ -268,7 +309,7 @@
         + rate_row(near_corner[2], near_edge[1, RATE], near_corner[3])
     )
 
-    @pl.loop(0, bands)
+    @pl.loop(0, bands, unroll=2)
     def _(b):
         index = band_at(coarse, b)
         wet = wet_at(b)
@@ -312,7 +353,7 @@
             put_band(resid, b, h - out)
             return flux_s
 
-        lax.fori_loop(0, bands, body, jnp.zeros((BAND, cols), jnp.float32))
+        lax.fori_loop(0, bands, body, jnp.zeros((BAND, cols), jnp.float32), unroll=2)
         for side in range(4):
             on_side(
                 side, lambda device, side=side: depth_copy(step, side, device, side).wait_recv()
@@ -332,7 +373,7 @@
     send_depth(0)
     route(0)
 
-    @pl.loop(0, bands)
+    @pl.loop(0, bands, unroll=2)
     def _(b):
         routed = band_at(resid, b)
         drained = band_at(coef_d, b) * power_five_thirds(routed)
@@ -347,6 +388,8 @@
         put_band(ponded, b, h)
         put_band(soak_out, b, soaked)
 
+    save_soak = pltpu.make_async_copy(soak_out, soak_out_hbm, save_sem.at[0])
+    save_soak.start()
     send_depth(1)
     route(1)
 
@@ -406,6 +449,8 @@
     total = lax.fori_loop(
         0, bands, drain, jnp.zeros((2 * blocks, REACH_BLOCK), jnp.float32)
     )
+    save_depth = pltpu.make_async_copy(depth_out, depth_out_hbm, save_sem.at[1])
+    save_depth.start()
     total = total[:blocks] + total[blocks:]
     for d in range(n_dev):
         totals[d] = total[d * per_dev : (d + 1) * per_dev]
@@ -432,30 +477,57 @@
         total_copy(offset).wait_recv()
 
     inflow_out[...] = jnp.sum(arrived[...], axis=0)
+    save_inflow = pltpu.make_async_copy(inflow_out, inflow_out_hbm, save_sem.at[2])
+    save_inflow.start()
+    save_soak.wait()
+    save_depth.wait()
+    save_inflow.wait()
 
     @pl.loop(1, n_dev)
     def _(offset):
         total_copy(offset).wait_send()
 
 
+def write_out(*refs):
+    sources, targets, held, load, save = refs[:3], refs[3:6], refs[6:9], refs[9], refs[10]
+    reads = [pltpu.make_async_copy(s, h, load.at[k]) for k, (s, h) in enumerate(zip(sources, held))]
+    writes = [pltpu.make_async_copy(h, t, save.at[k]) for k, (h, t) in enumerate(zip(held, targets))]
+    for read in reads:
+        read.start()
+    for read, write in zip(reads, writes):
+        read.wait()
+        write.start()
+    for write in writes:
+        write.wait()
+
+
 def shards(n_lat, n_lon, *operands):
     depth, order = operands[0], operands[9]
+    hbm = pl.BlockSpec(memory_space=pltpu.HBM)
     rows, cols = depth.shape
     tile_rows = operands[7].shape[0]
     n_dev = n_lat * n_lon
     per_dev = order.shape[0] // n_dev
-    vmem, smem = pl.BlockSpec(memory_space=pltpu.VMEM), pl.BlockSpec(memory_space=pltpu.SMEM)
     grid = pltpu.VMEM((rows, cols), jnp.float32)
-    return pl.pallas_call(
+    results = pl.pallas_call(
         functools.partial(kernel, n_lat, n_lon),
         out_shape=(
             jax.ShapeDtypeStruct((rows, cols), jnp.float32),
             jax.ShapeDtypeStruct((rows, cols), jnp.float32),
             jax.ShapeDtypeStruct((per_dev, REACH_BLOCK), jnp.float32),
         ),
-        in_specs=[vmem] * 5 + [smem, vmem, smem, vmem, smem],
-        out_specs=(vmem, vmem, vmem),
+        in_specs=[hbm] * 10,
+        out_specs=(hbm, hbm, hbm),
         scratch_shapes=[
+            (pltpu.SMEM if k in (5, 7, 9) else pltpu.VMEM)(x.shape, x.dtype)
+            for k, x in enumerate(operands)
+        ]
+        + [
+            grid,
+            grid,
+            pltpu.VMEM((per_dev, REACH_BLOCK), jnp.float32),
+            pltpu.SemaphoreType.DMA((10,)),
+            pltpu.SemaphoreType.DMA((3,)),
             pltpu.VMEM((tile_rows * BAND, cols), jnp.float32),
             grid,
             grid,
@@ -479,10 +551,20 @@
             pltpu.SemaphoreType.DMA((n_dev,)),
         ],
         compiler_params=pltpu.CompilerParams(
-            collective_id=0, has_side_effects=True, vmem_limit_bytes=40 * 1024 * 1024
+            collective_id=0, has_side_effects=True, vmem_limit_bytes=VMEM_LIMIT
         ),
         name="flow",
     )(*operands)
+    return pl.pallas_call(
+        write_out,
+        out_shape=[jax.ShapeDtypeStruct(x.shape, x.dtype) for x in results],
+        in_specs=[hbm] * 3,
+        out_specs=[hbm] * 3,
+        scratch_shapes=[pltpu.VMEM(x.shape, x.dtype) for x in results]
+        + [pltpu.SemaphoreType.DMA((3,)), pltpu.SemaphoreType.DMA((3,))],
+        compiler_params=pltpu.CompilerParams(vmem_limit_bytes=VMEM_LIMIT),
+        name="write",
+    )(*results)
 
 
 def solution(mesh):

time: 41.2 us -> 32 us (0.78)
  local copies, waits for them, and re-layouts: 10.6 us -> 0 us
  Pallas kernels: 29.6 us -> 31.2 us
    unnamed x23 -> x0, local copies, waits for them, and re-layouts: 10.6 us -> none
    pallas_call x0 -> x1, Pallas kernels: none -> 1.79 us  [shards(): pl.pallas_call(write_out, out_shape=[jax.ShapeDtypeStruct(x.shape, x.dtyp...]
where the time goes in v2:
time: 32 us; the launch traced here: 31.9 us
  Pallas kernels  31.2 us (98%)
  between operations  0.64 us (2%)
    pallas_call x1, Pallas kernels, shards(): pl.pallas_call(functools.partial(kernel, n_lat, n_lon), out_shape=(jax.Sh...  29.4 us
    pallas_call x1, Pallas kernels, shards(): pl.pallas_call(write_out, out_shape=[jax.ShapeDtypeStruct(x.shape, x.dtyp...  1.79 us

profile of v2, /device:TPU:0, one launch (start us, length us, event | category | flops | bytes accessed | tf_op | source)
XLA Modules:
  0.0 31.9 jit_solution(18024092541162386589)
XLA Ops:
  0.6 29.4 %flow.1 = (f32[128,512]{1,0:T(8,128)}, f32[128,512]{1,0:T(8,128)}, f32[2,128]{1,0:T(2,128)}) custom-call(f32[128,512]{1,0:T(8,128)} %depth_hbm.1, f32[128,512]{1,0:T(8,128)} %soakage_hbm.1, f32[128,512]{1,0:T(8,128)} %elevation_hbm.1, f32[128,512]{1,0:T(8,128)} %roughness_hbm.1, f32[128,512]{1,0:T(8,128)} %conductivity_hbm.1, f32[1,4]{1,0:T(1,128)} %runoff_hbm.1, ...), custom_call_target="tpu_custom_call" | custom-call | tf_op jit(solution)/shard_map/flow/pallas_call | solution.py:512
  30.1 1.8 %write.1 = (f32[128,512]{1,0:T(8,128)}, f32[128,512]{1,0:T(8,128)}, f32[2,128]{1,0:T(2,128)}) custom-call(f32[128,512]{1,0:T(8,128)} %get-tuple-element.6.refs_0_, f32[128,512]{1,0:T(8,128)} %get-tuple-element.7.refs_1_, f32[2,128]{1,0:T(2,128)} %get-tuple-element.8.refs_2_), custom_call_target="tpu_custom_call" | custom-call | tf_op jit(solution)/shard_map/write/pallas_call | solution.py:558

commit v3 on v2

--- a/solution.py
+++ b/solution.py
@@ -13,6 +13,7 @@
 LANES = 128
 BAND = 8
 PACK = 16
+PIECES = 4
 VMEM_LIMIT = 60 * 1024 * 1024
 MESH = pl.DeviceIdType.MESH
 
@@ -139,7 +140,7 @@
         device = lax.rem(me + offset, n_dev)
         return (lax.div(device, n_lon), lax.rem(device, n_lon))
 
-    @pl.loop(1, n_dev)
+    @pl.loop(1, n_dev, unroll=True)
     def _(offset):
         pl.semaphore_signal(barrier, inc=1, device_id=other(offset), device_id_type=MESH)
 
@@ -455,7 +456,7 @@
     for d in range(n_dev):
         totals[d] = total[d * per_dev : (d + 1) * per_dev]
 
-    @pl.loop(1, n_dev)
+    @pl.loop(1, n_dev, unroll=True)
     def _(offset):
         total_copy(offset).start()
 
@@ -472,7 +473,7 @@
                 ).wait_send(),
             )
 
-    @pl.loop(1, n_dev)
+    @pl.loop(1, n_dev, unroll=True)
     def _(offset):
         total_copy(offset).wait_recv()
 
@@ -483,15 +484,27 @@
     save_depth.wait()
     save_inflow.wait()
 
-    @pl.loop(1, n_dev)
+    @pl.loop(1, n_dev, unroll=True)
     def _(offset):
         total_copy(offset).wait_send()
 
 
+def pieces(results):
+    cuts = []
+    for k, x in enumerate(results):
+        count = PIECES if x.shape[0] % (PIECES * BAND) == 0 else 1
+        size = x.shape[0] // count
+        cuts += [(k, pl.ds(p * size, size)) for p in range(count)]
+    return cuts
+
+
 def write_out(*refs):
     sources, targets, held, load, save = refs[:3], refs[3:6], refs[6:9], refs[9], refs[10]
-    reads = [pltpu.make_async_copy(s, h, load.at[k]) for k, (s, h) in enumerate(zip(sources, held))]
-    writes = [pltpu.make_async_copy(h, t, save.at[k]) for k, (h, t) in enumerate(zip(held, targets))]
+    reads, writes = [], []
+    for n, (k, cut) in enumerate(pieces(sources)):
+        here = held[k].at[cut]
+        reads.append(pltpu.make_async_copy(sources[k].at[cut], here, load.at[n]))
+        writes.append(pltpu.make_async_copy(here, targets[k].at[cut], save.at[n]))
     for read in reads:
         read.start()
     for read, write in zip(reads, writes):
@@ -561,7 +574,7 @@
         in_specs=[hbm] * 3,
         out_specs=[hbm] * 3,
         scratch_shapes=[pltpu.VMEM(x.shape, x.dtype) for x in results]
-        + [pltpu.SemaphoreType.DMA((3,)), pltpu.SemaphoreType.DMA((3,))],
+        + [pltpu.SemaphoreType.DMA((len(pieces(results)),))] * 2,
         compiler_params=pltpu.CompilerParams(vmem_limit_bytes=VMEM_LIMIT),
         name="write",
     )(*results)

time: 32 us -> 31.9 us (level)
  no operation moved by 1% of the time
where the time goes in v3:
time: 31.9 us; the launch traced here: 31.7 us
  Pallas kernels  31 us (97%)
  between operations  0.64 us (2%)
    pallas_call x1, Pallas kernels, shards(): pl.pallas_call(functools.partial(kernel, n_lat, n_lon), out_shape=(jax.Sh...  29.2 us
    pallas_call x1, Pallas kernels, shards(): pl.pallas_call(write_out, out_shape=[jax.ShapeDtypeStruct(x.shape, x.dtyp...  1.85 us

profile of v3, /device:TPU:0, one launch (start us, length us, event | category | flops | bytes accessed | tf_op | source)
XLA Modules:
  0.0 31.7 jit_solution(8291854946269439607)
XLA Ops:
  0.6 29.2 %flow.1 = (f32[128,512]{1,0:T(8,128)}, f32[128,512]{1,0:T(8,128)}, f32[2,128]{1,0:T(2,128)}) custom-call(f32[128,512]{1,0:T(8,128)} %depth_hbm.1, f32[128,512]{1,0:T(8,128)} %soakage_hbm.1, f32[128,512]{1,0:T(8,128)} %elevation_hbm.1, f32[128,512]{1,0:T(8,128)} %roughness_hbm.1, f32[128,512]{1,0:T(8,128)} %conductivity_hbm.1, f32[1,4]{1,0:T(1,128)} %runoff_hbm.1, ...), custom_call_target="tpu_custom_call" | custom-call | tf_op jit(solution)/shard_map/flow/pallas_call | solution.py:525
  29.8 1.9 %write.1 = (f32[128,512]{1,0:T(8,128)}, f32[128,512]{1,0:T(8,128)}, f32[2,128]{1,0:T(2,128)}) custom-call(f32[128,512]{1,0:T(8,128)} %get-tuple-element.6.refs_0_, f32[128,512]{1,0:T(8,128)} %get-tuple-element.7.refs_1_, f32[2,128]{1,0:T(2,128)} %get-tuple-element.8.refs_2_), custom_call_target="tpu_custom_call" | custom-call | tf_op jit(solution)/shard_map/write/pallas_call | solution.py:571
